TPU v7x, 32 devices: a whole 2x2x4 slice. The times are simulated.
32 devices in a mesh: gx: 8 (over z, y), gy: 4 (over x, core).
Axes of the slice: x: 2, y: 2, z: 4, core: 2. Of those that a mesh axis runs over, the one named last changes fastest.
Arguments:
- tracers: float32 [10, 4, 256, 1024], P(None, None, 'gy', 'gx'), may hold values from -3.4 to 3.4
- kappa: float32 [4, 256, 1024], P(None, 'gy', 'gx'), may hold values from 0.00098 to 8
Outputs:
- diffused: float32 [10, 4, 256, 1024], P(None, None, 'gy', 'gx')
All inputs are finite; a program needn't handle non-finite values.
Results may differ from a plain program's by a relative error of at most 0.00055.
Values sent between devices are 32-bit elements; how exact they have to be, the bound alone decides.
A program may use at most 64 MiB of HBM per device.

v0:
```python
import functools

import jax
import jax.numpy as jnp
from jax import lax
from jax.experimental import pallas as pl
from jax.experimental.pallas import tpu as pltpu
from jax.sharding import PartitionSpec as P

RATE = 20000.0
RATE_Z = 0.05
SUB = 8
HALF = 0.5 * RATE


def merge(left, right):
    g_l, ef_l, el_l, kf_l, kl_l = left
    g_r, ef_r, el_r, kf_r, kl_r = right
    face = HALF * (kl_l + kf_r)
    e_p = el_l + g_l
    e_q = ef_r + g_r
    inverse = 1.0 / (e_p * e_q + face * (e_p + e_q))
    a_pp = (e_q + face) * inverse
    a_pq = face * inverse
    a_qq = (e_p + face) * inverse
    chain = (
        g_l * a_pq * g_r,
        ef_l + g_l * (el_l * a_pp + a_pq * ef_r),
        el_r + g_r * (ef_r * a_qq + a_pq * el_l),
        kf_l,
        kl_r,
    )
    return chain, (a_pp, a_pq, a_qq, g_l, g_r)


def middle(inverse, high):
    a_pp, a_pq, a_qq, g_l, g_r = inverse
    by_first = jnp.where(high, a_pq, a_pp) * g_l
    by_last = jnp.where(high, a_qq, a_pq) * g_r
    return by_first, by_last


def join_right(inverse, f_l, l_l, f_r, l_r):
    a_pp, a_pq, a_qq, g_l, g_r = inverse
    u = a_pp * l_l + a_pq * f_r
    v = a_pq * l_l + a_qq * f_r
    return f_l + g_l * u, l_r + g_r * v, u, v


def sublane_pair(value, level, high, axis):
    step = 1 << level
    low_side = jnp.where(high, pltpu.roll(value, step, axis), value)
    high_side = jnp.where(high, value, pltpu.roll(value, SUB - step, axis))
    return low_side, high_side


def high_bit(shape, axis, level):
    return (lax.broadcasted_iota(jnp.int32, shape, axis) & (1 << level)) != 0


def factor(kappa, cells, levels, message, tracers):
    planes, length = kappa.shape[0], kappa.shape[1]
    group = length // SUB
    k = [kappa[:, pl.ds(i, SUB, stride=group), :] for i in range(group)]
    coupling = HALF * (k[0] + k[1])
    first = jnp.ones_like(coupling)
    last = jnp.ones_like(coupling)
    for j in range(1, group - 1):
        face = HALF * (k[j] + k[j + 1])
        inverse = 1.0 / (last + coupling + face)
        to_first = coupling * inverse
        to_next = face * inverse
        cells[j, 0] = to_first
        cells[j, 1] = to_next
        cells[j, 2] = inverse
        first = first + to_first * last
        last = 1.0 + to_next * last
        coupling = coupling * to_next
    chain = (coupling, first, last, k[0], k[group - 1])
    for level in range(3):
        high = high_bit(coupling.shape, 1, level)
        pairs = [sublane_pair(value, level, high, 1) for value in chain]
        chain, inverse = merge([a for a, b in pairs], [b for a, b in pairs])
        for i, value in enumerate(inverse + middle(inverse, high)):
            levels[level, i] = value
    for i, value in enumerate(chain):
        for plane in range(planes):
            message[0, 2 * tracers + i, pl.ds(plane, 1), :] = value[plane, 0:1, :]


def eliminate(field, plane, cells, levels, kept, kept_levels, message):
    tracers, length = field.shape[0], field.shape[2]
    group = length // SUB

    def row(i):
        return field[:, plane, pl.ds(i, SUB, stride=group), :]

    first, last = row(0), row(1)
    for j in range(1, group - 1):
        kept[j, :, plane] = last
        first = first + cells[j, 0, plane] * last
        last = row(j + 1) + cells[j, 1, plane] * last
    for level in range(3):
        high = high_bit(first.shape, 1, level)
        inverse = [levels[level, i, plane] for i in range(5)]
        f_l, f_r = sublane_pair(first, level, high, 1)
        l_l, l_r = sublane_pair(last, level, high, 1)
        first, last, u, v = join_right(inverse, f_l, l_l, f_r, l_r)
        kept_levels[level, :, plane] = jnp.where(high, v, u)
    message[0, 0:tracers, pl.ds(plane, 1), :] = first[:, 0:1, :]
    message[0, tracers : 2 * tracers, pl.ds(plane, 1), :] = last[:, 0:1, :]


def back(field, plane, cells, levels, kept, kept_levels, ends):
    tracers, length = field.shape[0], field.shape[2]
    group = length // SUB
    shape = (tracers, SUB, field.shape[3])
    first = jnp.broadcast_to(ends[0:tracers, pl.ds(plane, 1), :], shape)
    last = jnp.broadcast_to(ends[tracers : 2 * tracers, pl.ds(plane, 1), :], shape)
    for level in reversed(range(3)):
        high = high_bit(shape, 1, level)
        inner = (
            kept_levels[level, :, plane]
            + levels[level, 5, plane] * first
            + levels[level, 6, plane] * last
        )
        first = jnp.where(high, inner, first)
        last = jnp.where(high, last, inner)
    field[:, plane, pl.ds(0, SUB, stride=group), :] = first
    field[:, plane, pl.ds(group - 1, SUB, stride=group), :] = last
    for j in reversed(range(1, group - 1)):
        last = (
            cells[j, 2, plane] * kept[j, :, plane]
            + cells[j, 0, plane] * first
            + cells[j, 1, plane] * last
        )
        field[:, plane, pl.ds(j, SUB, stride=group), :] = last


def partner(index, level):
    step = 1 << level
    return index + step - 2 * step * ((index // step) % 2)


def exchange(sizes, axis, message, received, ends, send_sems, recv_sems, cyclic):
    tracers = ends.shape[0] // 2
    index = {name: lax.axis_index(name) for name in sizes}
    me = index[axis]
    steps = []
    own = None
    for level in range(sizes[axis].bit_length() - 1):
        target = dict(index)
        target[axis] = partner(me, level)
        copy = pltpu.make_async_remote_copy(
            src_ref=message.at[level],
            dst_ref=received.at[level],
            send_sem=send_sems.at[level],
            recv_sem=recv_sems.at[level],
            device_id=tuple(target[name] for name in sizes),
            device_id_type=pl.DeviceIdType.MESH,
        )
        copy.start()
        high = (me // (1 << level)) % 2 == 1
        copy.wait()
        mine, other = message[level], received[level]
        left = jnp.where(high, other, mine)
        right = jnp.where(high, mine, other)
        chain, inverse = merge(
            [left[2 * tracers + i] for i in range(5)], [right[2 * tracers + i] for i in range(5)]
        )
        first, last, u, v = join_right(
            inverse,
            left[0:tracers],
            left[tracers : 2 * tracers],
            right[0:tracers],
            right[tracers : 2 * tracers],
        )
        steps.append((high, jnp.where(high, v, u)) + middle(inverse, high))
        own = (chain, first, last)
        if level + 1 < message.shape[0]:
            message[level + 1, 0:tracers] = first
            message[level + 1, tracers : 2 * tracers] = last
            for i in range(5):
                message[level + 1, 2 * tracers + i] = chain[i]
    (coupling, e_first, e_last, k_first, k_last), first, last = own
    if cyclic:
        coupling = coupling + HALF * (k_last + k_first)
    inverse = 1.0 / (e_first * e_last + coupling * (e_first + e_last))
    both = coupling * inverse
    first, last = (
        (e_last + coupling) * inverse * first + both * last,
        both * first + (e_first + coupling) * inverse * last,
    )
    for high, inner, by_first, by_last in reversed(steps):
        inner = inner + by_first * first + by_last * last
        first = jnp.where(high, inner, first)
        last = jnp.where(high, last, inner)
    ends[0:tracers] = first
    ends[tracers : 2 * tracers] = last


def kernel(
    sizes,
    tracers_ref,
    kappa_ref,
    out_ref,
    x_field,
    x_kappa,
    x_cells,
    x_levels,
    x_kept,
    x_kept_levels,
    x_message,
    x_received,
    x_ends,
    y_cells,
    y_levels,
    y_kept,
    y_kept_levels,
    y_message,
    y_received,
    y_ends,
    x_send,
    x_recv,
    y_send,
    y_recv,
):
    tracers, planes, rows, columns = tracers_ref.shape
    pairs = tracers // 2
    index = {name: lax.axis_index(name) for name in sizes}
    barrier = pltpu.get_barrier_semaphore()
    partners = 0
    for axis in sizes:
        for level in range(sizes[axis].bit_length() - 1):
            target = dict(index)
            target[axis] = partner(index[axis], level)
            pl.semaphore_signal(
                barrier,
                inc=1,
                device_id=tuple(target[name] for name in sizes),
                device_id_type=pl.DeviceIdType.MESH,
            )
            partners += 1

    for plane in range(planes):
        block = kappa_ref[plane]
        x_kappa[plane] = jnp.concatenate([block, block], 0).T
    factor(x_kappa, x_cells, x_levels, x_message, pairs)
    factor(kappa_ref, y_cells, y_levels, y_message, tracers)

    faces = [0.5 * RATE_Z * (kappa_ref[z] + kappa_ref[z + 1]) for z in range(planes - 1)]

    def load_pair(pair, carry):
        fields = [
            tracers_ref[pl.ds(2 * pair, 2), z].reshape(2 * rows, columns) for z in range(planes)
        ]
        flux = [
            jnp.concatenate([faces[z], faces[z]], 0) * (fields[z + 1] - fields[z])
            for z in range(planes - 1)
        ]
        for z in range(planes):
            start = fields[z]
            if z < planes - 1:
                start = start + flux[z]
            if z > 0:
                start = start - flux[z - 1]
            x_field[pair, z] = start.T
        return carry

    lax.fori_loop(0, pairs, load_pair, 0)

    def eliminate_x(plane, carry):
        eliminate(x_field, plane, x_cells, x_levels, x_kept, x_kept_levels, x_message)
        return carry

    for plane in range(planes):
        eliminate_x(plane, 0)
    pl.semaphore_wait(barrier, partners)
    exchange(sizes, "gx", x_message, x_received, x_ends, x_send, x_recv, True)
    for plane in range(planes):
        back(x_field, plane, x_cells, x_levels, x_kept, x_kept_levels, x_ends)

    def turn_pair(pair, carry):
        for z in range(planes):
            out_ref[pl.ds(2 * pair, 2), z] = x_field[pair, z].T.reshape(2, rows, columns)
        return carry

    lax.fori_loop(0, pairs, turn_pair, 0)
    for plane in range(planes):
        eliminate(out_ref, plane, y_cells, y_levels, y_kept, y_kept_levels, y_message)
    exchange(sizes, "gy", y_message, y_received, y_ends, y_send, y_recv, False)
    for plane in range(planes):
        back(out_ref, plane, y_cells, y_levels, y_kept, y_kept_levels, y_ends)


def shards(sizes, tracers, kappa):
    count, planes, rows, columns = tracers.shape
    pairs = count // 2
    lanes = 2 * rows

    def scratch(*shape):
        return pltpu.VMEM(shape, jnp.float32)

    def line(fields, length, width, axis):
        group = length // SUB
        hops = sizes[axis].bit_length() - 1
        message = (hops, 2 * fields + 5, planes, width)
        return [
            scratch(group, 3, planes, SUB, width),
            scratch(3, 7, planes, SUB, width),
            scratch(group, fields, planes, SUB, width),
            scratch(3, fields, planes, SUB, width),
            scratch(*message),
            scratch(*message),
            scratch(2 * fields, planes, width),
        ]

    hops_x = sizes["gx"].bit_length() - 1
    hops_y = sizes["gy"].bit_length() - 1
    return pl.pallas_call(
        functools.partial(kernel, sizes),
        out_shape=jax.ShapeDtypeStruct(tracers.shape, jnp.float32),
        in_specs=[pl.BlockSpec(memory_space=pltpu.VMEM)] * 2,
        out_specs=pl.BlockSpec(memory_space=pltpu.VMEM),
        scratch_shapes=[scratch(pairs, planes, columns, lanes), scratch(planes, columns, lanes)]
        + line(pairs, columns, lanes, "gx")
        + line(count, rows, columns, "gy")
        + [pltpu.SemaphoreType.DMA((hops,)) for hops in (hops_x, hops_x, hops_y, hops_y)],
        compiler_params=pltpu.CompilerParams(
            collective_id=0, has_side_effects=True, vmem_limit_bytes=40 * 1024 * 1024
        ),
    )(tracers, kappa)


def solution(mesh):
    sizes = {name: mesh.shape[name] for name in ("gx", "gy")}
    placed = (P(None, None, "gy", "gx"), P(None, "gy", "gx"))
    return jax.shard_map(
        functools.partial(shards, sizes),
        mesh=mesh,
        in_specs=placed,
        out_specs=P(None, None, "gy", "gx"),
        check_vma=False,
    )
```

profile of v0, /device:TPU:0, one launch (start us, length us, event | category | flops | bytes accessed | tf_op | source)
XLA Modules:
  0.0 25.8 jit_solution(3385614052798420325)
XLA Ops:
  0.0 0.0 copy-start
  0.0 1.3 %copy-done = f32[10,4,64,128]{3,2,1,0:T(8,128)S(1)} copy-done((f32[10,4,64,128]{3,2,1,0:T(8,128)S(1)}, f32[10,4,64,128]{3,2,1,0:T(8,128)}, u32[]{:S(2)}) %copy-start) | copy-done | bytes 1310744
  1.3 0.0 copy-start.1
  1.3 0.9 %copy-done.1 = f32[4,64,128]{2,1,0:T(8,128)S(1)} copy-done((f32[4,64,128]{2,1,0:T(8,128)S(1)}, f32[4,64,128]{2,1,0:T(8,128)}, u32[]{:S(2)}) %copy-start.1) | copy-done | bytes 131096
  2.2 22.5 %shard_map.28 = f32[10,4,64,128]{3,2,1,0:T(8,128)S(1)} custom-call(f32[10,4,64,128]{3,2,1,0:T(8,128)S(1)} %copy-done, f32[4,64,128]{2,1,0:T(8,128)S(1)} %copy-done.1), custom_call_target="tpu_custom_call" | custom-call | tf_op jit(solution)/shard_map/pallas_call | solution.py:320
  24.7 1.1 %copy.4 = f32[10,4,64,128]{3,2,1,0:T(8,128)} copy(f32[10,4,64,128]{3,2,1,0:T(8,128)S(1)} %shard_map.28) | data formatting | bytes 2621440
Async XLA Ops:
  0.0 1.3 %copy-start = (f32[10,4,64,128]{3,2,1,0:T(8,128)S(1)}, f32[10,4,64,128]{3,2,1,0:T(8,128)}, u32[]{:S(2)}) copy-start(f32[10,4,64,128]{3,2,1,0:T(8,128)} %tracers_ref.1) | copy-start | bytes 3932164
  1.3 0.9 %copy-start.1 = (f32[4,64,128]{2,1,0:T(8,128)S(1)}, f32[4,64,128]{2,1,0:T(8,128)}, u32[]{:S(2)}) copy-start(f32[4,64,128]{2,1,0:T(8,128)} %kappa_ref.1) | copy-start | bytes 393220
where the time goes:
time: 26 us; the launch traced here: 25.8 us
  Pallas kernels  22.5 us (87%)
  local copies, waits for them, and re-layouts  3.28 us (13%)
    pallas_call x1, Pallas kernels, shards(): pl.pallas_call(functools.partial(kernel, sizes), out_shape=jax.ShapeDtype...  22.5 us
    unnamed x5, local copies, waits for them, and re-layouts  3.28 us

commit v1 on v0

v1 whole, which is shorter than its diff:
```python
import functools

import jax
import jax.numpy as jnp
from jax import lax
from jax.experimental import pallas as pl
from jax.experimental.pallas import tpu as pltpu
from jax.sharding import PartitionSpec as P

RATE = 20000.0
RATE_Z = 0.05
SUB = 8
HALF = 0.5 * RATE


def merge(left, right):
    g_l, ef_l, el_l, kf_l, kl_l = left
    g_r, ef_r, el_r, kf_r, kl_r = right
    face = HALF * (kl_l + kf_r)
    e_p = el_l + g_l
    e_q = ef_r + g_r
    inverse = 1.0 / (e_p * e_q + face * (e_p + e_q))
    a_pp = (e_q + face) * inverse
    a_pq = face * inverse
    a_qq = (e_p + face) * inverse
    chain = (
        g_l * a_pq * g_r,
        ef_l + g_l * (el_l * a_pp + a_pq * ef_r),
        el_r + g_r * (ef_r * a_qq + a_pq * el_l),
        kf_l,
        kl_r,
    )
    return chain, (a_pp, a_pq, a_qq, g_l, g_r)


def middle(inverse, high):
    a_pp, a_pq, a_qq, g_l, g_r = inverse
    by_first = jnp.where(high, a_pq, a_pp) * g_l
    by_last = jnp.where(high, a_qq, a_pq) * g_r
    return by_first, by_last


def join_right(inverse, f_l, l_l, f_r, l_r):
    a_pp, a_pq, a_qq, g_l, g_r = inverse
    u = a_pp * l_l + a_pq * f_r
    v = a_pq * l_l + a_qq * f_r
    return f_l + g_l * u, l_r + g_r * v, u, v


def sublane_pair(value, level, high, axis):
    step = 1 << level
    low_side = jnp.where(high, pltpu.roll(value, step, axis), value)
    high_side = jnp.where(high, value, pltpu.roll(value, SUB - step, axis))
    return low_side, high_side


def high_bit(shape, axis, level):
    return (lax.broadcasted_iota(jnp.int32, shape, axis) & (1 << level)) != 0


def factor(kappa, cells, levels, message):
    planes, length = kappa.shape[0], kappa.shape[1]
    group = length // SUB
    k = [kappa[:, pl.ds(i, SUB, stride=group), :] for i in range(group)]
    coupling = HALF * (k[0] + k[1])
    first = jnp.ones_like(coupling)
    last = jnp.ones_like(coupling)
    for j in range(1, group - 1):
        face = HALF * (k[j] + k[j + 1])
        inverse = 1.0 / (last + coupling + face)
        to_first = coupling * inverse
        to_next = face * inverse
        cells[j, 0] = to_first
        cells[j, 1] = to_next
        cells[j, 2] = inverse
        first = first + to_first * last
        last = 1.0 + to_next * last
        coupling = coupling * to_next
    chain = (coupling, first, last, k[0], k[group - 1])
    for level in range(3):
        high = high_bit(coupling.shape, 1, level)
        pairs = [sublane_pair(value, level, high, 1) for value in chain]
        chain, inverse = merge([a for a, b in pairs], [b for a, b in pairs])
        for i, value in enumerate(inverse + middle(inverse, high)):
            levels[level, i] = value
    for i, value in enumerate(chain):
        for plane in range(planes):
            message[0, i, pl.ds(plane, 1), :] = value[plane, 0:1, :]


def eliminate(field, part, plane, cells, levels, kept, kept_levels, message):
    start, count = part
    group = field.shape[2] // SUB
    fields = pl.ds(start, count)

    def row(i):
        return field[fields, plane, pl.ds(i, SUB, stride=group), :]

    first, last = row(0), row(1)
    for j in range(1, group - 1):
        kept[j, fields, plane] = last
        first = first + cells[j, 0, plane] * last
        last = row(j + 1) + cells[j, 1, plane] * last
    for level in range(3):
        high = high_bit(first.shape, 1, level)
        inverse = [levels[level, i, plane] for i in range(5)]
        f_l, f_r = sublane_pair(first, level, high, 1)
        l_l, l_r = sublane_pair(last, level, high, 1)
        first, last, u, v = join_right(inverse, f_l, l_l, f_r, l_r)
        kept_levels[level, fields, plane] = jnp.where(high, v, u)
    message[0, 0:count, pl.ds(plane, 1), :] = first[:, 0:1, :]
    message[0, count : 2 * count, pl.ds(plane, 1), :] = last[:, 0:1, :]


def back(field, part, plane, cells, levels, kept, kept_levels, ends):
    start, count = part
    group = field.shape[2] // SUB
    fields = pl.ds(start, count)
    shape = (count, SUB, field.shape[3])
    first = jnp.broadcast_to(ends[0:count, pl.ds(plane, 1), :], shape)
    last = jnp.broadcast_to(ends[count : 2 * count, pl.ds(plane, 1), :], shape)
    for level in reversed(range(3)):
        high = high_bit(shape, 1, level)
        inner = (
            kept_levels[level, fields, plane]
            + levels[level, 5, plane] * first
            + levels[level, 6, plane] * last
        )
        first = jnp.where(high, inner, first)
        last = jnp.where(high, last, inner)
    field[fields, plane, pl.ds(0, SUB, stride=group), :] = first
    field[fields, plane, pl.ds(group - 1, SUB, stride=group), :] = last
    for j in reversed(range(1, group - 1)):
        last = (
            cells[j, 2, plane] * kept[j, fields, plane]
            + cells[j, 0, plane] * first
            + cells[j, 1, plane] * last
        )
        field[fields, plane, pl.ds(j, SUB, stride=group), :] = last


def flipped(index, bits):
    level = 0
    target = index
    while (1 << level) <= bits:
        step = 1 << level
        if bits & step:
            target = target + step - 2 * step * ((index // step) % 2)
        level += 1
    return target


def device(sizes, axis, bits):
    index = {name: lax.axis_index(name) for name in sizes}
    index[axis] = flipped(index[axis], bits)
    return tuple(index[name] for name in sizes)


def send(sizes, axis, buffer, send_sems, recv_sems, row):
    copies = []
    for bits in range(1, sizes[axis]):
        copy = pltpu.make_async_remote_copy(
            src_ref=buffer.at[0],
            dst_ref=buffer.at[bits],
            send_sem=send_sems.at[row, bits],
            recv_sem=recv_sems.at[row, bits],
            device_id=device(sizes, axis, bits),
            device_id_type=pl.DeviceIdType.MESH,
        )
        copy.start()
        copies.append(copy)
    return copies


def halves(value, high):
    value = value.reshape((value.shape[0] // 2, 2) + value.shape[1:])
    even, odd = value[:, 0], value[:, 1]
    return jnp.where(high, odd, even), jnp.where(high, even, odd)


def join_coefficients(sizes, axis, buffer, cyclic):
    me = lax.axis_index(axis)
    chain = [buffer[:, i] for i in range(5)]
    steps = []
    for level in range(sizes[axis].bit_length() - 1):
        high = (me // (1 << level)) % 2 == 1
        pairs = [halves(value, high) for value in chain]
        chain, inverse = merge([a for a, b in pairs], [b for a, b in pairs])
        steps.append((high, inverse, middle([value[0] for value in inverse], high)))
    coupling, e_first, e_last, k_first, k_last = [value[0] for value in chain]
    if cyclic:
        coupling = coupling + HALF * (k_last + k_first)
    inverse = 1.0 / (e_first * e_last + coupling * (e_first + e_last))
    closing = (
        (e_last + coupling) * inverse,
        coupling * inverse,
        (e_first + coupling) * inverse,
    )
    return steps, closing


def find_ends(joined, buffer, ends):
    steps, closing = joined
    count = ends.shape[0] // 2
    first, last = buffer[:, 0:count], buffer[:, count : 2 * count]
    inner_parts = []
    for high, inverse, weights in steps:
        f_l, f_r = halves(first, high)
        l_l, l_r = halves(last, high)
        first, last, u, v = join_right([value[:, None] for value in inverse], f_l, l_l, f_r, l_r)
        inner_parts.append(jnp.where(high, v[0], u[0]))
    first, last = first[0], last[0]
    first, last = (
        closing[0] * first + closing[1] * last,
        closing[1] * first + closing[2] * last,
    )
    for (high, inverse, weights), inner in reversed(list(zip(steps, inner_parts))):
        inner = inner + weights[0] * first + weights[1] * last
        first = jnp.where(high, inner, first)
        last = jnp.where(high, last, inner)
    ends[0:count] = first
    ends[count : 2 * count] = last


def kernel(sizes, parts, tracers_hbm, kappa_hbm, out_ref, *scratch):
    pieces = len(parts)
    tracers_ref, kappa_ref, x_field, x_kappa = scratch[:4]
    scratch = scratch[4:]
    x_cells, x_levels, x_kept, x_kept_levels, x_coef = scratch[:5]
    x_buffers, x_ends = scratch[5 : 5 + pieces], scratch[5 + pieces : 5 + 2 * pieces]
    scratch = scratch[5 + 2 * pieces :]
    y_cells, y_levels, y_kept, y_kept_levels, y_coef = scratch[:5]
    y_buffers, y_ends = scratch[5 : 5 + pieces], scratch[5 + pieces : 5 + 2 * pieces]
    x_send, x_recv, y_send, y_recv, in_sems = scratch[5 + 2 * pieces :]
    tracers, planes, rows, columns = tracers_ref.shape
    y_parts = [(2 * start, 2 * count) for start, count in parts]

    barrier = pltpu.get_barrier_semaphore()
    partners = 0
    for axis in sizes:
        for bits in reversed(range(1, sizes[axis])):
            pl.semaphore_signal(
                barrier,
                inc=1,
                device_id=device(sizes, axis, bits),
                device_id_type=pl.DeviceIdType.MESH,
            )
            partners += 1
    kappa_copy = pltpu.make_async_copy(kappa_hbm, kappa_ref, in_sems.at[pieces])
    kappa_copy.start()
    loads = []
    for piece, (start, count) in enumerate(y_parts):
        block = pl.ds(start, count)
        load = pltpu.make_async_copy(
            tracers_hbm.at[block], tracers_ref.at[block], in_sems.at[piece]
        )
        load.start()
        loads.append(load)

    kappa_copy.wait()
    for plane in range(planes):
        block = kappa_ref[plane]
        x_kappa[plane] = jnp.concatenate([block, block], 0).T
    factor(x_kappa, x_cells, x_levels, x_coef)
    factor(kappa_ref, y_cells, y_levels, y_coef)

    faces = [0.5 * RATE_Z * (kappa_ref[z] + kappa_ref[z + 1]) for z in range(planes - 1)]

    def load_pair(pair, carry):
        fields = [
            tracers_ref[pl.ds(2 * pair, 2), z].reshape(2 * rows, columns) for z in range(planes)
        ]
        flux = [
            jnp.concatenate([faces[z], faces[z]], 0) * (fields[z + 1] - fields[z])
            for z in range(planes - 1)
        ]
        for z in range(planes):
            start = fields[z]
            if z < planes - 1:
                start = start + flux[z]
            if z > 0:
                start = start - flux[z - 1]
            x_field[pair, z] = start.T
        return carry

    for piece, (start, count) in enumerate(parts):
        loads[piece].wait()
        lax.fori_loop(start, start + count, load_pair, 0)
        for plane in range(planes):
            eliminate(
                x_field,
                parts[piece],
                plane,
                x_cells,
                x_levels,
                x_kept,
                x_kept_levels,
                x_buffers[piece],
            )
    pl.semaphore_wait(barrier, partners)
    x_copies = [send(sizes, "gx", x_coef, x_send, x_recv, pieces)]
    for piece in range(pieces):
        x_copies.append(send(sizes, "gx", x_buffers[piece], x_send, x_recv, piece))
    y_copies = [send(sizes, "gy", y_coef, y_send, y_recv, pieces)]
    for copy in x_copies[0]:
        copy.wait()
    x_joined = join_coefficients(sizes, "gx", x_coef, True)
    for copy in y_copies[0]:
        copy.wait()
    y_joined = join_coefficients(sizes, "gy", y_coef, False)

    def turn_pair(pair, carry):
        for z in range(planes):
            out_ref[pl.ds(2 * pair, 2), z] = x_field[pair, z].T.reshape(2, rows, columns)
        return carry

    for piece, (start, count) in enumerate(parts):
        for copy in x_copies[piece + 1]:
            copy.wait()
        find_ends(x_joined, x_buffers[piece], x_ends[piece])
        for plane in range(planes):
            back(
                x_field,
                parts[piece],
                plane,
                x_cells,
                x_levels,
                x_kept,
                x_kept_levels,
                x_ends[piece],
            )
        lax.fori_loop(start, start + count, turn_pair, 0)
        for plane in range(planes):
            eliminate(
                out_ref,
                y_parts[piece],
                plane,
                y_cells,
                y_levels,
                y_kept,
                y_kept_levels,
                y_buffers[piece],
            )
        y_copies.append(send(sizes, "gy", y_buffers[piece], y_send, y_recv, piece))
    for piece in range(pieces):
        for copy in y_copies[piece + 1]:
            copy.wait()
        find_ends(y_joined, y_buffers[piece], y_ends[piece])
        for plane in range(planes):
            back(
                out_ref,
                y_parts[piece],
                plane,
                y_cells,
                y_levels,
                y_kept,
                y_kept_levels,
                y_ends[piece],
            )


def shards(sizes, tracers, kappa):
    count, planes, rows, columns = tracers.shape
    pairs = count // 2
    lanes = 2 * rows
    early = (pairs + 1) // 2
    parts = [(0, early), (early, pairs - early)]

    def scratch(*shape):
        return pltpu.VMEM(shape, jnp.float32)

    def line(each, length, width, axis):
        fields = each * pairs
        group = length // SUB
        size = sizes[axis]
        return (
            [
                scratch(group, 3, planes, SUB, width),
                scratch(3, 7, planes, SUB, width),
                scratch(group, fields, planes, SUB, width),
                scratch(3, fields, planes, SUB, width),
                scratch(size, 5, planes, width),
            ]
            + [scratch(size, 2 * each * number, planes, width) for _, number in parts]
            + [scratch(2 * each * number, planes, width) for _, number in parts]
        )

    semaphores = [
        pltpu.SemaphoreType.DMA((len(parts) + 1, sizes[axis])) for axis in ("gx", "gx", "gy", "gy")
    ]
    return pl.pallas_call(
        functools.partial(kernel, sizes, parts),
        out_shape=jax.ShapeDtypeStruct(tracers.shape, jnp.float32),
        in_specs=[pl.BlockSpec(memory_space=pltpu.HBM)] * 2,
        out_specs=pl.BlockSpec(memory_space=pltpu.VMEM),
        scratch_shapes=[
            scratch(*tracers.shape),
            scratch(*kappa.shape),
            scratch(pairs, planes, columns, lanes),
            scratch(planes, columns, lanes),
        ]
        + line(1, columns, lanes, "gx")
        + line(2, rows, columns, "gy")
        + semaphores
        + [pltpu.SemaphoreType.DMA((len(parts) + 1,))],
        compiler_params=pltpu.CompilerParams(
            collective_id=0, has_side_effects=True, vmem_limit_bytes=48 * 1024 * 1024
        ),
    )(tracers, kappa)


def solution(mesh):
    sizes = {name: mesh.shape[name] for name in ("gx", "gy")}
    placed = (P(None, None, "gy", "gx"), P(None, "gy", "gx"))
    return jax.shard_map(
        functools.partial(shards, sizes),
        mesh=mesh,
        in_specs=placed,
        out_specs=P(None, None, "gy", "gx"),
        check_vma=False,
    )
```

time: 26 us -> 21.5 us (0.83)
  Pallas kernels: 22.5 us -> 18 us
    pallas_call x1, Pallas kernels: 22.5 us -> 18 us  [shards(): pl.pallas_call(functools.partial(kernel, sizes, parts), out_shape=jax.Sha...]
where the time goes in v1:
time: 21.5 us; the launch traced here: 21.3 us
  Pallas kernels  18 us (84%)
  local copies, waits for them, and re-layouts  3.28 us (15%)
    pallas_call x1, Pallas kernels, shards(): pl.pallas_call(functools.partial(kernel, sizes, parts), out_shape=jax.Sha...  18 us
    unnamed x5, local copies, waits for them, and re-layouts  3.28 us

profile of v1, /device:TPU:0, one launch (start us, length us, event | category | flops | bytes accessed | tf_op | source)
XLA Modules:
  0.0 21.3 jit_solution(9853864264618314632)
XLA Ops:
  0.0 0.0 copy-start
  0.0 1.3 %copy-done = f32[10,4,64,128]{3,2,1,0:T(8,128)S(1)} copy-done((f32[10,4,64,128]{3,2,1,0:T(8,128)S(1)}, f32[10,4,64,128]{3,2,1,0:T(8,128)}, u32[]{:S(2)}) %copy-start) | copy-done | bytes 1310744
  1.3 0.0 copy-start.1
  1.3 0.9 %copy-done.1 = f32[4,64,128]{2,1,0:T(8,128)S(1)} copy-done((f32[4,64,128]{2,1,0:T(8,128)S(1)}, f32[4,64,128]{2,1,0:T(8,128)}, u32[]{:S(2)}) %copy-start.1) | copy-done | bytes 131096
  2.2 18.0 %shard_map.28 = f32[10,4,64,128]{3,2,1,0:T(8,128)S(1)} custom-call(f32[10,4,64,128]{3,2,1,0:T(8,128)S(1)} %copy-done, f32[4,64,128]{2,1,0:T(8,128)S(1)} %copy-done.1), custom_call_target="tpu_custom_call" | custom-call | tf_op jit(solution)/shard_map/pallas_call | solution.py:391
  20.3 1.1 %copy.4 = f32[10,4,64,128]{3,2,1,0:T(8,128)} copy(f32[10,4,64,128]{3,2,1,0:T(8,128)S(1)} %shard_map.28) | data formatting | bytes 2621440
Async XLA Ops:
  0.0 1.3 %copy-start = (f32[10,4,64,128]{3,2,1,0:T(8,128)S(1)}, f32[10,4,64,128]{3,2,1,0:T(8,128)}, u32[]{:S(2)}) copy-start(f32[10,4,64,128]{3,2,1,0:T(8,128)} %tracers_hbm.1) | copy-start | bytes 3932164
  1.3 0.9 %copy-start.1 = (f32[4,64,128]{2,1,0:T(8,128)S(1)}, f32[4,64,128]{2,1,0:T(8,128)}, u32[]{:S(2)}) copy-start(f32[4,64,128]{2,1,0:T(8,128)} %kappa_hbm.1) | copy-start | bytes 393220

commit v2 on v1

--- a/solution.py
+++ b/solution.py
@@ -262,7 +262,6 @@
         block = kappa_ref[plane]
         x_kappa[plane] = jnp.concatenate([block, block], 0).T
     factor(x_kappa, x_cells, x_levels, x_coef)
-    factor(kappa_ref, y_cells, y_levels, y_coef)
 
     faces = [0.5 * RATE_Z * (kappa_ref[z] + kappa_ref[z + 1]) for z in range(planes - 1)]
 
@@ -283,6 +282,7 @@
             x_field[pair, z] = start.T
         return carry
 
+    x_copies = []
     for piece, (start, count) in enumerate(parts):
         loads[piece].wait()
         lax.fori_loop(start, start + count, load_pair, 0)
@@ -297,17 +297,15 @@
                 x_kept_levels,
                 x_buffers[piece],
             )
-    pl.semaphore_wait(barrier, partners)
-    x_copies = [send(sizes, "gx", x_coef, x_send, x_recv, pieces)]
-    for piece in range(pieces):
+        if piece == 0:
+            pl.semaphore_wait(barrier, partners)
+            x_copies.append(send(sizes, "gx", x_coef, x_send, x_recv, pieces))
         x_copies.append(send(sizes, "gx", x_buffers[piece], x_send, x_recv, piece))
+    factor(kappa_ref, y_cells, y_levels, y_coef)
     y_copies = [send(sizes, "gy", y_coef, y_send, y_recv, pieces)]
     for copy in x_copies[0]:
         copy.wait()
     x_joined = join_coefficients(sizes, "gx", x_coef, True)
-    for copy in y_copies[0]:
-        copy.wait()
-    y_joined = join_coefficients(sizes, "gy", y_coef, False)
 
     def turn_pair(pair, carry):
         for z in range(planes):
@@ -342,6 +340,9 @@
                 y_buffers[piece],
             )
         y_copies.append(send(sizes, "gy", y_buffers[piece], y_send, y_recv, piece))
+    for copy in y_copies[0]:
+        copy.wait()
+    y_joined = join_coefficients(sizes, "gy", y_coef, False)
     for piece in range(pieces):
         for copy in y_copies[piece + 1]:
             copy.wait()
@@ -363,8 +364,7 @@
     count, planes, rows, columns = tracers.shape
     pairs = count // 2
     lanes = 2 * rows
-    early = (pairs + 1) // 2
-    parts = [(0, early), (early, pairs - early)]
+    parts = [(0, 1)] + [(start, min(2, pairs - start)) for start in range(1, pairs, 2)]
 
     def scratch(*shape):
         return pltpu.VMEM(shape, jnp.float32)
@@ -404,7 +404,7 @@
         + semaphores
         + [pltpu.SemaphoreType.DMA((len(parts) + 1,))],
         compiler_params=pltpu.CompilerParams(
-            collective_id=0, has_side_effects=True, vmem_limit_bytes=48 * 1024 * 1024
+            collective_id=0, has_side_effects=True, vmem_limit_bytes=52 * 1024 * 1024
         ),
     )(tracers, kappa)
 

time: 21.5 us -> 19.5 us (0.907)
  local copies, waits for them, and re-layouts: 3.28 us -> 1.96 us
  Pallas kernels: 18 us -> 17.3 us
    unnamed x5 -> x3, local copies, waits for them, and re-layouts: 3.28 us -> 1.96 us
    pallas_call x1, Pallas kernels: 18 us -> 17.3 us  [shards(): pl.pallas_call(functools.partial(kernel, sizes, parts), out_shape=jax.Sha...]
where the time goes in v2:
time: 19.5 us; the launch traced here: 19.3 us
  Pallas kernels  17.3 us (89%)
  local copies, waits for them, and re-layouts  1.96 us (10%)
    pallas_call x1, Pallas kernels, shards(): pl.pallas_call(functools.partial(kernel, sizes, parts), out_shape=jax.Sha...  17.3 us
    unnamed x3, local copies, waits for them, and re-layouts  1.96 us

profile of v2, /device:TPU:0, one launch (start us, length us, event | category | flops | bytes accessed | tf_op | source)
XLA Modules:
  0.0 19.3 jit_solution(2872613399518762684)
XLA Ops:
  0.0 0.0 copy-start
  0.0 0.9 %copy-done = f32[4,64,128]{2,1,0:T(8,128)S(1)} copy-done((f32[4,64,128]{2,1,0:T(8,128)S(1)}, f32[4,64,128]{2,1,0:T(8,128)}, u32[]{:S(2)}) %copy-start) | copy-done | bytes 131096
  0.9 17.3 %shard_map.28 = f32[10,4,64,128]{3,2,1,0:T(8,128)S(1)} custom-call(f32[10,4,64,128]{3,2,1,0:T(8,128)} %tracers_hbm.1, f32[4,64,128]{2,1,0:T(8,128)S(1)} %copy-done), custom_call_target="tpu_custom_call" | custom-call | tf_op jit(solution)/shard_map/pallas_call | solution.py:391
  18.3 1.1 %copy.4 = f32[10,4,64,128]{3,2,1,0:T(8,128)} copy(f32[10,4,64,128]{3,2,1,0:T(8,128)S(1)} %shard_map.28) | data formatting | bytes 2621440
Async XLA Ops:
  0.0 0.9 %copy-start = (f32[4,64,128]{2,1,0:T(8,128)S(1)}, f32[4,64,128]{2,1,0:T(8,128)}, u32[]{:S(2)}) copy-start(f32[4,64,128]{2,1,0:T(8,128)} %kappa_hbm.1) | copy-start | bytes 393220
